TPU v7x, 32 devices: a whole 2x2x4 slice. The times are simulated.
32 devices in a mesh: seq: 8 (over z, x), head: 4 (over y, core).
Axes of the slice: x: 2, y: 2, z: 4, core: 2. Of those that a mesh axis runs over, the one named last changes fastest.
Arguments:
- tokens: bfloat16 [8192, 1024], P('seq', 'head'), may hold values from -6 to 6
- lengths: int32 [3], replicated, may hold values from 256 to 7168, as said below
- norm1_gain: float32 [1024], replicated, may hold values from 0.25 to 1.75
- w_mixer: bfloat16 [1024, 6144], P(None, 'head'), may hold values from -0.1875 to 0.1875
- w_rates: bfloat16 [1024, 24], P(None, 'head'), may hold values from -0.1875 to 0.1875
- decay_log: float32 [8], P('head'), may hold values from -20 to -2
- rates_bias: float32 [24], P('head'), may hold values from -12 to 1
- conv_weight: float32 [4, 5120], P(None, 'head'), may hold values from -2.5 to 2.5
- out_gain: float32 [128], replicated, may hold values from 0.25 to 1.75
- w_out: bfloat16 [1024, 1024], P('head'), may hold values from -0.1875 to 0.1875
- norm2_gain: float32 [1024], replicated, may hold values from 0.25 to 1.75
- w_ffn_gate: bfloat16 [1024, 2816], P(None, 'head'), may hold values from -0.1875 to 0.1875
- w_ffn_up: bfloat16 [1024, 2816], P(None, 'head'), may hold values from -0.1875 to 0.1875
- w_ffn_down: bfloat16 [2816, 1024], P('head'), may hold values from -0.109375 to 0.109375
- out_grad: bfloat16 [8192, 1024], P('seq', 'head'), may hold values from -6 to 6
Outputs:
- output: bfloat16 [8192, 1024], P('seq', 'head')
- tokens_grad: bfloat16 [8192, 1024], P('seq', 'head')
- norm1_gain_grad: float32 [1024], replicated
- w_mixer_grad: float32 [1024, 6144], P('seq', 'head')
- w_rates_grad: float32 [1024, 24], P('seq', 'head')
- decay_log_grad: float32 [8], P('head')
- rates_bias_grad: float32 [24], P('head')
- conv_weight_grad: float32 [4, 5120], P(None, 'head')
- out_gain_grad: float32 [128], replicated
- w_out_grad: float32 [1024, 1024], P('head', 'seq')
- norm2_gain_grad: float32 [1024], replicated
- w_ffn_gate_grad: float32 [1024, 2816], P('seq', 'head')
- w_ffn_up_grad: float32 [1024, 2816], P('seq', 'head')
- w_ffn_down_grad: float32 [2816, 1024], P('head', 'seq')
Inputs may be any that keep to these rules, and one draw needn't show every extreme that they name: 3 document lengths summing to 8192; the middle one is 7168; the first and the last sum to 1024, each 256 or more.
All inputs are finite; a program needn't handle non-finite values.
Results may differ from a plain program's by a relative error of at most 0.019.
Values may be sent and summed in bfloat16 or wider, within the bound.
No kernel may reach another device: no remote copies, remote signals or barrier semaphores. Data moves between devices by JAX's collectives and lax.ppermute only.
A program may use at most 192 MiB of HBM per device.

v0:
```python
import jax
import jax.numpy as jnp
from jax import lax
from jax.sharding import PartitionSpec as P

DK = 128
DV = 128
NH = 2
CONV = 4
GROUP = 64
QKV = 640
MIXW = 768


EPS = 1e-06
HIGH = lax.Precision.HIGHEST


def shifted(value, axis, steps):
    count = lax.axis_size(axis)
    first, last = (max(0, -steps), min(count, count - steps))
    return lax.ppermute(value, axis, [(source, source + steps) for source in range(first, last)])


def prefix_2(value, axis, join, neutral):
    count, mine = (lax.axis_size(axis), lax.axis_index(axis))
    pieces = jax.tree.map(lambda part: lax.all_gather(part, axis), value)
    so_far = jax.tree.map(
        lambda part, zero: jnp.full_like(part, 0) + jnp.asarray(zero, part.dtype), value, neutral
    )

    def prefix_step(position, so_far):
        longer = join(so_far, jax.tree.map(lambda part: part[position], pieces))
        return jax.tree.map(lambda new, old: jnp.where(position < mine, new, old), longer, so_far)

    return lax.fori_loop(0, count - 1, prefix_step, so_far)


def carried_in(shard, axis, combine, identity):
    count, position = (lax.axis_size(axis), lax.axis_index(axis))
    everything = jax.tree.map(
        lambda part, kind: lax.all_gather(part.astype(kind), axis),
        shard,
        jax.tree.map(lambda a: jnp.bfloat16 if a.dtype == jnp.float32 else a.dtype, shard),
    )
    start = jax.tree.map(
        lambda part, zero: jnp.broadcast_to(jnp.asarray(zero, part.dtype), part.shape),
        shard,
        identity,
    )

    def carried_step(k, before):
        at = count - 1 - k
        reached = at > position
        new = combine(
            before, jax.tree.map(lambda part, own: part[at].astype(own.dtype), everything, shard)
        )
        return jax.tree.map(lambda a, b: jnp.where(reached, a, b), new, before)

    return lax.fori_loop(0, count, carried_step, start)


def mix(pattern, leading, trailing):
    return jnp.einsum(pattern, leading, trailing, precision=HIGH)


def dot_t(leading, trailing):
    return lax.dot_general(
        leading, trailing, (((1,), (1,)), ((), ())), preferred_element_type=jnp.float32
    )


def t_dot(leading, trailing):
    return lax.dot_general(
        leading, trailing, (((0,), (0,)), ((), ())), preferred_element_type=jnp.float32
    )


def compose(earlier, following):
    return (
        mix("hij,hjk->hik", following[0], earlier[0]),
        mix("hij,hjk->hik", following[0], earlier[1]) + following[1],
    )


def norm_back(grad_unit, unit_rows, inv_scale):
    return inv_scale * (
        grad_unit - unit_rows * jnp.mean(grad_unit * unit_rows, axis=-1, keepdims=True)
    )


def prepare(ext_pre, conv_w, rates_raw, decay_w, bias_w, doc_ext):
    tok_rows = rates_raw.shape[0]
    heads_local = decay_w.shape[0]
    taps = conv_w.reshape(CONV, heads_local, QKV)
    doc_here = doc_ext[CONV - 1 :]
    mixed = jnp.zeros((tok_rows, heads_local, QKV), jnp.float32)
    for offset in range(CONV):
        start_row = CONV - 1 - offset
        same_doc = (doc_ext[start_row : start_row + tok_rows] == doc_here)[:, None, None]
        mixed = (
            mixed
            + jnp.where(same_doc, ext_pre[start_row : start_row + tok_rows], 0.0) * taps[start_row]
        )
    active = jax.nn.silu(mixed)
    query = active[:, :, :DK]
    keys = active[:, :, DK : DK + NH * DK].reshape(tok_rows, heads_local, NH, DK)
    values = active[:, :, DK + NH * DK :].reshape(tok_rows, heads_local, NH, DV)
    query = query * lax.rsqrt(jnp.sum(query * query, axis=-1, keepdims=True) + EPS)
    keys = keys * lax.rsqrt(jnp.sum(keys * keys, axis=-1, keepdims=True) + EPS)
    logits = (rates_raw + bias_w).reshape(tok_rows, heads_local, NH + 1)
    betas = jax.nn.sigmoid(logits[:, :, :NH])
    log_gate = -jnp.exp(decay_w) * jax.nn.softplus(logits[:, :, NH])
    return (query, keys, values, betas, log_gate)


def to_substeps(query, keys, values, betas, log_gate):
    tok_rows, heads_local = log_gate.shape
    total = tok_rows * NH
    key_sub = jnp.transpose(keys, (1, 0, 2, 3)).reshape(heads_local, total, DK)
    value_sub = jnp.transpose(values, (1, 0, 2, 3)).reshape(heads_local, total, DV)
    beta_sub = jnp.transpose(betas, (1, 0, 2)).reshape(heads_local, total)
    nothing = jnp.zeros_like(log_gate)
    gate_steps = jnp.stack([log_gate] + [nothing] * (NH - 1), axis=-1)
    gate_sub = jnp.transpose(gate_steps, (1, 0, 2)).reshape(heads_local, total)
    blank = jnp.zeros_like(query)
    query_steps = jnp.stack([blank] * (NH - 1) + [query], axis=2)
    query_sub = jnp.transpose(query_steps, (1, 0, 2, 3)).reshape(heads_local, total, DK)
    return (query_sub, key_sub, value_sub, beta_sub, gate_sub)


def group_pass(sub_steps, doc_sub, prev_doc, state):
    query_sub, key_sub, value_sub, beta_sub, gate_sub = sub_steps
    heads_local, total = beta_sub.shape
    blocks = total // GROUP

    def split(array):
        shaped = array.reshape((heads_local, blocks, GROUP) + array.shape[2:])
        return jnp.moveaxis(shaped, 1, 0)

    block_docs = doc_sub.reshape(blocks, GROUP)
    before = jnp.concatenate([jnp.reshape(prev_doc, (1,)), block_docs[:-1, GROUP - 1]])
    row_ids = lax.broadcasted_iota(jnp.int32, (GROUP, GROUP), 0)
    col_ids = lax.broadcasted_iota(jnp.int32, (GROUP, GROUP), 1)
    unit_diag = jnp.eye(GROUP, dtype=jnp.float32)

    def advance(carry, inputs):
        query_c, key_c, value_c, beta_c, gate_c, docs_c, before_c = inputs
        cumul = jnp.cumsum(gate_c, axis=-1)
        same = docs_c[:, None] == docs_c[None, :]
        inclusive = same & (row_ids >= col_ids)
        strictly = same & (row_ids > col_ids)
        spread = cumul[:, :, None] - cumul[:, None, :]
        decay = jnp.where(inclusive, jnp.exp(jnp.where(inclusive, spread, 0.0)), 0.0)
        opening = jnp.where(docs_c == before_c, jnp.exp(cumul), 0.0)
        key_key = mix("hid,hjd->hij", key_c, key_c)
        below_diag = jnp.where(strictly, beta_c[:, :, None] * decay * key_key, 0.0)
        target = beta_c[:, :, None] * (
            value_c - opening[:, :, None] * mix("hid,hdw->hiw", key_c, carry)
        )
        deltas = jax.vmap(
            lambda system, right_side: jax.scipy.linalg.solve_triangular(
                system, right_side, lower=True, unit_diagonal=True
            )
        )(unit_diag + below_diag, target)
        query_key = mix("hid,hjd->hij", query_c, key_c)
        outputs = opening[:, :, None] * mix("hid,hdw->hiw", query_c, carry) + mix(
            "hij,hjw->hiw", decay * query_key, deltas
        )
        closing = decay[:, GROUP - 1, :]
        updated = opening[:, GROUP - 1][:, None, None] * carry + mix(
            "hjd,hjw->hdw", key_c * closing[:, :, None], deltas
        )
        return (updated, outputs)

    final, outputs = lax.scan(
        advance,
        state,
        (
            split(query_sub),
            split(key_sub),
            split(value_sub),
            split(beta_sub),
            split(gate_sub),
            block_docs,
            before,
        ),
    )
    outputs = jnp.moveaxis(outputs, 0, 1).reshape(heads_local, total, outputs.shape[-1])
    return (outputs, final)


def last_step(out_sub, tok_rows):
    heads_local, total, width = out_sub.shape
    return out_sub.reshape(heads_local, tok_rows, NH, width)[:, :, NH - 1]


def local(
    tokens,
    lengths,
    norm1_gain,
    w_mixer,
    w_rates,
    decay_log,
    rates_bias,
    conv_weight,
    out_gain,
    w_out,
    norm2_gain,
    w_ffn_gate,
    w_ffn_up,
    w_ffn_down,
    out_grad,
):
    tok_rows, col_share = tokens.shape
    heads_local = decay_log.shape[0]
    seq_place = lax.axis_index("seq")
    head_place = lax.axis_index("head")
    col_start = head_place * col_share
    doc_ends = jnp.cumsum(lengths)
    places = seq_place * tok_rows - (CONV - 1) + jnp.arange(tok_rows + CONV - 1, dtype=jnp.int32)
    doc_ext = jnp.sum((places[:, None] >= doc_ends[None, :]).astype(jnp.int32), axis=1)
    doc_ext = jnp.where(places < 0, -1, doc_ext)
    doc_sub = jnp.repeat(doc_ext[CONV - 1 :], NH)
    prev_doc = doc_ext[CONV - 2]

    def mixer_local(ext_pre, conv_w, rates_raw, decay_w, bias_w, state):
        prepared = prepare(ext_pre, conv_w, rates_raw, decay_w, bias_w, doc_ext)
        out_sub, end_state = group_pass(to_substeps(*prepared), doc_sub, prev_doc, state)
        return (jnp.transpose(last_step(out_sub, tok_rows), (1, 0, 2)), end_state)

    whole_rows = lax.all_gather(tokens, "head", axis=1, tiled=True)
    x_full = whole_rows.astype(jnp.float32)
    scale_one = lax.rsqrt(jnp.mean(x_full * x_full, axis=-1, keepdims=True) + EPS)
    unit_one = x_full * scale_one
    h_one = (unit_one * norm1_gain).astype(jnp.bfloat16)
    raw_mix = jnp.dot(h_one, w_mixer, preferred_element_type=jnp.float32).reshape(
        tok_rows, heads_local, MIXW
    )
    rates_raw = jnp.dot(h_one, w_rates, preferred_element_type=jnp.float32)
    pre_conv = raw_mix[:, :, :QKV]
    gate_o = raw_mix[:, :, QKV:]
    rim_rows = shifted(pre_conv[tok_rows - (CONV - 1) :], "seq", 1)
    ext_pre = jnp.concatenate([rim_rows, pre_conv], axis=0)
    prepared = prepare(ext_pre, conv_weight, rates_raw, decay_log, rates_bias, doc_ext)
    query_sub, key_sub, value_sub, beta_sub, gate_sub = to_substeps(*prepared)
    wide_values = jnp.concatenate(
        [value_sub, jnp.zeros((heads_local, value_sub.shape[1], DK), jnp.float32)], axis=-1
    )
    eye_heads = jnp.broadcast_to(jnp.eye(DK, dtype=jnp.float32), (heads_local, DK, DK))
    start_state = jnp.concatenate(
        [jnp.zeros((heads_local, DK, DV), jnp.float32), eye_heads], axis=-1
    )
    out_wide, end_wide = group_pass(
        (query_sub, key_sub, wide_values, beta_sub, gate_sub), doc_sub, prev_doc, start_state
    )
    carried = end_wide[:, :, :DV]
    transfer = end_wide[:, :, DV:]
    identity = (eye_heads, jnp.zeros((heads_local, DK, DV), jnp.float32))
    prefix = prefix_2((transfer, carried), "seq", compose, identity)
    state_in = prefix[1]
    picked = last_step(out_wide, tok_rows)
    attn_heads = picked[:, :, :DV] + mix("htk,hkw->htw", picked[:, :, DV:], state_in)
    attn = jnp.transpose(attn_heads, (1, 0, 2))
    scale_o = lax.rsqrt(jnp.mean(attn * attn, axis=-1, keepdims=True) + EPS)
    unit_o = attn * scale_o
    sig_o = jax.nn.sigmoid(gate_o)
    silu_o = gate_o * sig_o
    normed_b = (unit_o * out_gain * silu_o).reshape(tok_rows, heads_local * DV).astype(jnp.bfloat16)
    branch_part = jnp.dot(normed_b, w_out, preferred_element_type=jnp.float32)
    branch = lax.psum(branch_part.astype(jnp.bfloat16), "head").astype(jnp.float32)
    resid = x_full + branch
    scale_two = lax.rsqrt(jnp.mean(resid * resid, axis=-1, keepdims=True) + EPS)
    unit_two = resid * scale_two
    h_two = (unit_two * norm2_gain).astype(jnp.bfloat16)
    resid_own = lax.dynamic_slice_in_dim(resid, col_start, col_share, 1)
    gate_f = jnp.dot(h_two, w_ffn_gate, preferred_element_type=jnp.float32)
    up_f = jnp.dot(h_two, w_ffn_up, preferred_element_type=jnp.float32)
    sig_f = jax.nn.sigmoid(gate_f)
    silu_f = gate_f * sig_f
    act_b = (silu_f * up_f).astype(jnp.bfloat16)
    ffn_share = lax.psum_scatter(
        jnp.dot(act_b, w_ffn_down, preferred_element_type=jnp.float32).astype(jnp.bfloat16),
        "head",
        scatter_dimension=1,
        tiled=True,
    ).astype(jnp.float32)
    output = (resid_own + ffn_share).astype(jnp.bfloat16)
    grad_full = lax.all_gather(out_grad, "head", axis=1, tiled=True)
    grad_act = dot_t(grad_full, w_ffn_down)
    grad_down = t_dot(act_b, grad_full)
    grad_gate = (grad_act * up_f * sig_f * (1.0 + gate_f * (1.0 - sig_f))).astype(jnp.bfloat16)
    grad_up = (grad_act * silu_f).astype(jnp.bfloat16)
    grad_wgate = t_dot(h_two, grad_gate)
    grad_wup = t_dot(h_two, grad_up)
    grad_h_two_part = dot_t(grad_gate, w_ffn_gate) + dot_t(grad_up, w_ffn_up)
    grad_h_two = lax.psum(grad_h_two_part.astype(jnp.bfloat16), "head").astype(jnp.float32)
    grad_norm2 = jnp.sum(grad_h_two * unit_two, axis=0)
    grad_resid = grad_full.astype(jnp.float32) + norm_back(
        grad_h_two * norm2_gain, unit_two, scale_two
    )
    grad_branch = grad_resid.astype(jnp.bfloat16)
    grad_wout = t_dot(normed_b, grad_branch)
    grad_normed = dot_t(grad_branch, w_out).reshape(tok_rows, heads_local, DV)
    grad_gate_o = grad_normed * unit_o * out_gain * sig_o * (1.0 + gate_o * (1.0 - sig_o))
    grad_scaled = grad_normed * silu_o
    grad_outgain = jnp.sum(grad_scaled * unit_o, axis=(0, 1))
    grad_attn = norm_back(grad_scaled * out_gain, unit_o, scale_o)
    state_grad_here = mix("htk,thw->hkw", picked[:, :, DV:], grad_attn)
    flipped = jnp.swapaxes(transfer, 1, 2)
    suffix = carried_in((flipped, state_grad_here), "seq", compose, identity)
    (redone, end_again), pull = jax.vjp(
        mixer_local, ext_pre, conv_weight, rates_raw, decay_log, rates_bias, state_in
    )
    grad_ext, grad_conv, grad_rates_f, grad_decay, grad_bias, spare = pull((grad_attn, suffix[1]))
    rim_grad = shifted(grad_ext[: CONV - 1], "seq", -1)
    grad_pre = grad_ext[CONV - 1 :] + jnp.concatenate(
        [jnp.zeros((tok_rows - (CONV - 1), heads_local, QKV), jnp.float32), rim_grad], axis=0
    )
    grad_raw = (
        jnp.concatenate([grad_pre, grad_gate_o], axis=-1)
        .reshape(tok_rows, heads_local * MIXW)
        .astype(jnp.bfloat16)
    )
    grad_rates = grad_rates_f.astype(jnp.bfloat16)
    grad_wmixer = t_dot(h_one, grad_raw)
    grad_wrates = t_dot(h_one, grad_rates)
    grad_h_part = dot_t(grad_raw, w_mixer) + dot_t(grad_rates, w_rates)
    grad_h_one, grad_outgain_all = (
        lax.psum(grad_h_part.astype(jnp.bfloat16), "head").astype(jnp.float32),
        lax.psum(grad_outgain.astype(jnp.bfloat16), "head").astype(jnp.float32),
    )
    grad_norm1 = jnp.sum(grad_h_one * unit_one, axis=0)
    grad_tokens = grad_resid + norm_back(grad_h_one * norm1_gain, unit_one, scale_one)
    tokens_grad = lax.dynamic_slice_in_dim(grad_tokens, col_start, col_share, 1).astype(
        jnp.bfloat16
    )
    small = lax.psum(
        (grad_norm1, grad_outgain_all, grad_norm2, grad_decay, grad_bias, grad_conv), "seq"
    )
    gain_one_grad = small[0]
    gain_out_grad = small[1]
    gain_two_grad = small[2]
    decay_grad = small[3]
    bias_grad = small[4]
    conv_grad = small[5]
    weight_all = (
        lax.psum_scatter(
            grad_wmixer.astype(jnp.bfloat16), "seq", scatter_dimension=0, tiled=True
        ).astype(jnp.float32),
        lax.psum_scatter(
            grad_wrates.astype(jnp.bfloat16), "seq", scatter_dimension=0, tiled=True
        ).astype(jnp.float32),
        lax.psum_scatter(
            grad_wout.astype(jnp.bfloat16), "seq", scatter_dimension=1, tiled=True
        ).astype(jnp.float32),
        lax.psum_scatter(
            grad_wgate.astype(jnp.bfloat16), "seq", scatter_dimension=0, tiled=True
        ).astype(jnp.float32),
        lax.psum_scatter(
            grad_wup.astype(jnp.bfloat16), "seq", scatter_dimension=0, tiled=True
        ).astype(jnp.float32),
        lax.psum_scatter(
            grad_down.astype(jnp.bfloat16), "seq", scatter_dimension=1, tiled=True
        ).astype(jnp.float32),
    )
    return (
        output,
        tokens_grad,
        gain_one_grad,
        weight_all[0],
        weight_all[1],
        decay_grad,
        bias_grad,
        conv_grad,
        gain_out_grad,
        weight_all[2],
        gain_two_grad,
        weight_all[3],
        weight_all[4],
        weight_all[5],
    )


def solution(mesh):
    placed = (
        P("seq", "head"),
        P(),
        P(),
        P(None, "head"),
        P(None, "head"),
        P("head"),
        P("head"),
        P(None, "head"),
        P(),
        P("head", None),
        P(),
        P(None, "head"),
        P(None, "head"),
        P("head", None),
        P("seq", "head"),
    )
    return jax.shard_map(
        local,
        mesh=mesh,
        in_specs=placed,
        out_specs=(
            P("seq", "head"),
            P("seq", "head"),
            P(),
            P("seq", "head"),
            P("seq", "head"),
            P("head"),
            P("head"),
            P(None, "head"),
            P(),
            P("head", "seq"),
            P(),
            P("seq", "head"),
            P("seq", "head"),
            P("head", "seq"),
        ),
        check_vma=False,
    )
```

profile of v0, /device:TPU:0, one launch (start us, length us, event | category | flops | bytes accessed | tf_op | source)
XLA Modules:
  0.0 3989.3 jit_solution(5260510551720291725)
XLA Ops:
  13.7 21.5 all-gather.9.cloned.1.call-done
  74.9 12.6 fusion.193
  120.8 713.3 %while.132 = (s32[]{:T(128)}, f32[2,128,256]{2,1,0:T(8,128)S(1)}, f32[32,2,64,256]{3,2,1,0:T(8,128)}, s32[32,64]{1,0:T(8,128)}, s32[32]{0:T(128)}, /*index=5*/f3...) while((s32[]{:T(128)}, f32[2,128,256]{2,1,0:T(8,128)S(1)}, ...), condition=%wide.region_7.8_spmd.clone, body=%wide.region_5.7_spmd.clone.sunk | while | flops 226984064 | bytes 2951209 | solution.py:176
  845.9 28.3 all-gather.13.cloned.1.call-done
  874.3 41.6 %all-gather.15.cloned.1.call-done = f32[16,128,128]{2,1,0:T(8,128)} async-done(((f32[2,128,128]{2,1,0:T(8,128)}), f32[16,128,128]{2,1,0:T(8,128)}) %all-gather.15.cloned.1.call-update) | async-done | bytes 1048592 | tf_op jit(solution)/shard_map/all_gather | solution.py:27
  938.0 33.5 all-gather.2
  971.5 14.2 all-reduce.26.cloned.1.call-done
  997.2 12.9 all-gather.11.cloned.1.call-done
  1024.6 1160.4 %while.133 = (s32[]{:T(128)}, f32[2,128,128]{2,1,0:T(8,128)S(1)}, pred[32,2,64,64]{3,2,1,0:T(32,128)(4,1)}, f32[32,2,64,64]{3,2,1,0:T(8,128)}, f32[32,2,64]{2,1,...) while((s32[]{:T(128)}, f32[2,128,128]{2,1,0:T(8,128)S(1)}, ...), condition=%wide.region_21.22_spmd.clone, body=%wide.region_19.21_spmd.clone.sunk | while | flops 113647872 | bytes 2918981 | solution.py:176
  1035.1 11.2 custom-call.60
  1071.3 11.2 custom-call.60
  1143.8 11.2 custom-call.60
  1180.0 11.2 custom-call.60
  1252.5 11.2 custom-call.60
  1288.8 11.2 custom-call.60
  1361.1 11.2 custom-call.60
  1397.4 11.2 custom-call.60
  1433.7 11.2 custom-call.60
  1470.0 11.2 custom-call.60
  1506.2 11.2 custom-call.60
  1578.6 11.2 custom-call.60
  2206.6 33.4 all-gather.3
  2258.7 1158.2 %while.134 = (s32[]{:T(128)}, f32[2,128,128]{2,1,0:T(8,128)S(1)}, f32[32,2,64,128]{3,2,0,1:T(8,128)}, f32[32,2,64,128]{3,2,0,1:T(8,128)}, f32[32,2,64,128]{3,2,0...) while((s32[]{:T(128)}, f32[2,128,128]{2,1,0:T(8,128)S(1)}, ...), condition=%wide.region_32.33_spmd.clone, body=%wide.region_22.32_spmd.clone.sunk | while | flops 258732096 | bytes 5188657 | solution.py:176
  3451.1 14.2 multiply_reduce_fusion.3
  3553.0 60.5 %reduce-scatter.24.cloned.1.call-done = bf16[128,256]{1,0:T(8,128)(2,1)} async-done(((bf16[1024,256]{1,0:T(8,128)(2,1)}), bf16[128,256]{1,0:T(8,128)(2,1)}) %reduce-scatter.24.cloned.1.call-update) | async-done | bytes 65552
  3615.1 51.3 %all-reduce.30.cloned.1.call-done = bf16[1024,1024]{1,0:T(8,128)(2,1)} async-done(((bf16[1024,1024]{1,0:T(8,128)(2,1)}), bf16[1024,1024]{1,0:T(8,128)(2,1)}) %all-reduce.30.cloned.1.call-update) | async-done | bytes 2097168 | tf_op jit(solution)/shard_map/psum | solution.py:330
  3673.2 38.2 all-reduce.21
  3714.4 20.5 reduce-scatter.26.cloned.1.call-done
  3736.7 65.8 %reduce-scatter.28.cloned.1.call-done = bf16[128,704]{1,0:T(8,128)(2,1)} async-done(((bf16[1024,704]{1,0:T(8,128)(2,1)}), bf16[128,704]{1,0:T(8,128)(2,1)}) %reduce-scatter.28.cloned.1.call-update) | async-done | bytes 180240
  3804.4 65.3 %reduce-scatter.30.cloned.1.call-done = bf16[128,704]{1,0:T(8,128)(2,1)} async-done(((bf16[1024,704]{1,0:T(8,128)(2,1)}), bf16[128,704]{1,0:T(8,128)(2,1)}) %reduce-scatter.30.cloned.1.call-update) | async-done | bytes 180240
  3871.5 31.3 reduce-scatter.18.cloned.1.call-done
  3905.1 75.3 %reduce-scatter.20.cloned.1.call-done = bf16[128,1536]{1,0:T(8,128)(2,1)} async-done(((bf16[1024,1536]{1,0:T(8,128)(2,1)}), bf16[128,1536]{1,0:T(8,128)(2,1)}) %reduce-scatter.20.cloned.1.call-update) | async-done | bytes 393232 | tf_op jit(solution)/shard_map/reduce_scatter | solution.py:348
  (3170 shorter events, 3227.1 us)
Async XLA Ops:
  7.2 31.2 copy-start
  7.2 30.2 copy-start.66
  7.2 30.2 copy-start.56
  7.2 30.2 copy-start.75
  7.2 28.0 all-gather.9.cloned.1.call-start
  8.0 866.3 %all-gather.13.cloned.1.call-start = ((), (), s32[]{:S(2)}) async-start(), calls=%async_computation.14 | async-start | bytes 1179648 | tf_op jit(solution)/shard_map/all_gather | solution.py:27
  10.7 64.1 %copy-start.44 = (f32[2,640]{1,0:T(2,128)}, f32[2,640]{1,0:T(2,128)S(1)}, u32[]{:S(2)}) copy-start(f32[2,640]{1,0:T(2,128)S(1)} %mul.1000) | copy-start | bytes 15364
  10.7 64.1 %copy-start.46 = (f32[2,640]{1,0:T(2,128)}, f32[2,640]{1,0:T(2,128)S(1)}, u32[]{:S(2)}) copy-start(f32[2,640]{1,0:T(2,128)S(1)} %mul.1003) | copy-start | bytes 15364
  10.8 64.1 %copy-start.48 = (f32[2,640]{1,0:T(2,128)}, f32[2,640]{1,0:T(2,128)S(1)}, u32[]{:S(2)}) copy-start(f32[2,640]{1,0:T(2,128)S(1)} %mul.1006) | copy-start | bytes 15364
  10.8 64.0 %copy-start.50 = (f32[2,640]{1,0:T(2,128)}, f32[2,640]{1,0:T(2,128)S(1)}, u32[]{:S(2)}) copy-start(f32[2,640]{1,0:T(2,128)S(1)} %mul.1009) | copy-start | bytes 15364
  13.6 44.2 %copy-start.68 = (f32[2]{0:T(128)}, f32[2]{0:T(128)S(1)}, u32[]{:S(2)}) copy-start(f32[2]{0:T(128)S(1)} %exponential_negate_fusion) | copy-start | bytes 28
  13.7 61.2 %copy-start.58 = (pred[1024]{0:T(1024)(128)(4,1)}, pred[1024]{0:T(1024)(128)(4,1)S(1)}, u32[]{:S(2)}) copy-start(pred[1024]{0:T(1024)(128)(4,1)S(1)} %get-tuple-element.2650) | copy-start | bytes 3076
  13.7 61.2 %copy-start.60 = (pred[1024]{0:T(1024)(128)(4,1)}, pred[1024]{0:T(1024)(128)(4,1)S(1)}, u32[]{:S(2)}) copy-start(pred[1024]{0:T(1024)(128)(4,1)S(1)} %get-tuple-element.2651) | copy-start | bytes 3076
  13.7 61.2 %copy-start.62 = (pred[1024]{0:T(1024)(128)(4,1)}, pred[1024]{0:T(1024)(128)(4,1)S(1)}, u32[]{:S(2)}) copy-start(pred[1024]{0:T(1024)(128)(4,1)S(1)} %get-tuple-element.2652) | copy-start | bytes 3076
  54.4 20.4 collective-permute-start
  91.4 17.4 copy-start.40
  834.9 81.0 %all-gather.15.cloned.1.call-start = ((), (), s32[]{:S(2)}) async-start(), calls=%async_computation.15 | async-start | bytes 1179648 | tf_op jit(solution)/shard_map/all_gather | solution.py:27
  835.6 150.1 %all-reduce.26.cloned.1.call-start = ((), (), s32[]{:S(2)}) async-start(), calls=%async_computation.8 | async-start | bytes 4194304 | tf_op jit(solution)/shard_map/psum | solution.py:271
  935.4 74.7 %all-gather.11.cloned.1.call-start = ((), (), s32[]{:S(2)}) async-start(), calls=%async_computation.10 | async-start | bytes 2621440 | tf_op jit(solution)/shard_map/all_gather | solution.py:289
  936.0 1248.9 %all-reduce.28.cloned.1.call-start = ((), (), s32[]{:S(2)}) async-start(), calls=%async_computation.11 | async-start | bytes 4194304 | tf_op jit(solution)/shard_map/psum | solution.py:297
  971.5 17.3 copy-start.52
  1023.5 2528.0 %reduce-scatter.22.cloned.1.call-start = ((), (), s32[]{:S(2)}) async-start(), calls=%async_computation.16 | async-start | bytes 294912
  3451.1 14.3 copy-start.45
  3451.1 14.3 copy-start.47
  3478.6 13.3 collective-permute-start.1
  3486.9 126.5 %reduce-scatter.24.cloned.1.call-start = ((), (), s32[]{:S(2)}) async-start(), calls=%async_computation.17 | async-start | bytes 589824
  3491.8 174.5 %all-reduce.30.cloned.1.call-start = ((), (), s32[]{:S(2)}) async-start(), calls=%async_computation.12 | async-start | bytes 4194304 | tf_op jit(solution)/shard_map/psum | solution.py:330
  3508.9 226.0 %reduce-scatter.26.cloned.1.call-start = ((), (), s32[]{:S(2)}) async-start(), calls=%async_computation.18 | async-start | bytes 1769472
  3516.7 285.8 %reduce-scatter.28.cloned.1.call-start = ((), (), s32[]{:S(2)}) async-start(), calls=%async_computation.19 | async-start | bytes 1769472
  3524.2 345.5 %reduce-scatter.30.cloned.1.call-start = ((), (), s32[]{:S(2)}) async-start(), calls=%async_computation.20 | async-start | bytes 1769472
  3531.7 371.1 %reduce-scatter.18.cloned.1.call-start = ((), (), s32[]{:S(2)}) async-start(), calls=%async_computation.9 | async-start | bytes 2621440 | tf_op jit(solution)/shard_map/reduce_scatter | solution.py:282
  3536.7 443.7 %reduce-scatter.20.cloned.1.call-start = ((), (), s32[]{:S(2)}) async-start(), calls=%async_computation.13 | async-start | bytes 3538944 | tf_op jit(solution)/shard_map/reduce_scatter | solution.py:348
  (187 other events, 704.0 us)
Sparse Core Ops, SparseCore 0:
  9.6 25.5 all-gather.8
  835.0 39.2 all-gather.12
  877.0 38.8 all-gather.14
  935.5 50.1 all-reduce.25
  987.2 22.8 all-gather.10
  1023.6 51.4 all-reduce.27
  3487.1 61.4 reduce-scatter.21
  3552.5 60.9 reduce-scatter.23
  3615.9 50.4 all-reduce.29
  3669.6 65.1 reduce-scatter.25
  3738.7 63.8 reduce-scatter.27
  3805.8 63.8 reduce-scatter.29
  3872.3 30.3 reduce-scatter.17
  3906.2 74.1 reduce-scatter.19
where the time goes:
time: 4050 us; the launch traced here: 3990 us
  other arithmetic  1530 us (38%)
  matrix products  1250 us (31%)
  local copies, waits for them, and re-layouts  574 us (14%)
  waiting for transfers between devices  491 us (12%)
  blocking collectives  111 us (3%)
    another operation x384, other arithmetic, advance(): jax.scipy.linalg.solve_triangular(system, right_side, lower=True, unit_di...  1040 us
    dot_general x753, matrix products, mix(): return jnp.einsum(pattern, leading, trailing, precision=HIGH)  1020 us
    unnamed x19, waiting for transfers between devices  214 us
    dynamic_update_slice x224, local copies, waits for them, and re-layouts, group_pass(): lax.scan(advance, state, (split(query_sub), split(key_sub), split(value_s...  191 us
    another operation x128, matrix products, advance(): jax.scipy.linalg.solve_triangular(system, right_side, lower=True, unit_di...  127 us
    dynamic_update_slice x96, other arithmetic, group_pass(): lax.scan(advance, state, (split(query_sub), split(key_sub), split(value_s...  107 us
    eq x64, other arithmetic, advance(): opening = jnp.where(docs_c == before_c, jnp.exp(cumul), 0.0)  85.3 us
  transfers between devices with their start and end apart: 16, of which 12 were waited for; matrix products, arithmetic and copies ran while one was open for 32% of the time, Pallas kernels for 0%

commit v1 on v0

v1 whole, which is shorter than its diff:
```python
import functools

import jax
import jax.numpy as jnp
from jax import lax
from jax.experimental import pallas as pl
from jax.experimental.pallas import tpu as pltpu
from jax.sharding import PartitionSpec as P

DK = 128
DV = 128
NH = 2
CONV = 4
QKV = 640
MIXW = 768
EPS = 1e-06

CHUNK = 64
SPAN = 128
ROWS = 256
LEVELS = 6
HALO = 16

F32 = jnp.float32
BF16 = jnp.bfloat16

NN = (((1,), (0,)), ((), ()))
NT = (((1,), (1,)), ((), ()))
TN = (((0,), (0,)), ((), ()))

P_INV = 3
P_FWD = 3
P_STATE = 3
P_BWD = 3


def halves(value):
    high = value.astype(BF16)
    return high, (value - high.astype(F32)).astype(BF16)


def mm(left, right, dims=NN, passes=1):
    if passes == 1:
        return lax.dot_general(
            left.astype(BF16), right.astype(BF16), dims, preferred_element_type=F32
        )
    if passes == 6:
        return lax.dot_general(
            left, right, dims, precision=lax.Precision.HIGHEST, preferred_element_type=F32
        )
    left_h, left_l = halves(left)
    right_h, right_l = halves(right)
    dot = functools.partial(lax.dot_general, dimension_numbers=dims, preferred_element_type=F32)
    return dot(left_h, right_h) + (dot(left_h, right_l) + dot(left_l, right_h))


def iota(shape, axis):
    return lax.broadcasted_iota(jnp.int32, shape, axis)


def doc_of(place, marks, ends):
    count = jnp.zeros_like(place)
    for j in range(ends):
        count = count + jnp.where(place >= marks[1 + j], 1, 0)
    return jnp.where(place < 0, -1, count)


def doc_scalar(place, marks, ends):
    count = jnp.int32(0)
    for j in range(ends):
        count = count + (place >= marks[1 + j]).astype(jnp.int32)
    return jnp.where(place < 0, -1, count)


def conv_masks(start, marks, ends, rows, direction):
    place = start + iota((rows, DK), 0)
    here = doc_of(place, marks, ends)
    return [None] + [
        doc_of(place + direction * s, marks, ends) == here for s in range(1, CONV)
    ]


def softplus(v):
    return jnp.maximum(v, 0.0) + jnp.log1p(jnp.exp(-jnp.abs(v)))


def chunk_sum_matrix(upper):
    row, col = iota((SPAN, SPAN), 0), iota((SPAN, SPAN), 1)
    keep = (col >= row) if upper else (col <= row)
    keep = keep & ((row // CHUNK) == (col // CHUNK))
    return jnp.where(keep, 1.0, 0.0).astype(F32)


def part_columns(h, part):
    begin = h * QKV + part * DK
    return slice(begin, begin + DK)


def convolved(ext, conv, masks, h, part):
    cols = part_columns(h, part)
    total = ext[8 : 8 + SPAN, cols] * conv[CONV - 1 : CONV, cols]
    for s in range(1, CONV):
        moved = jnp.where(masks[s], ext[8 - s : 8 - s + SPAN, cols], 0.0)
        total = total + moved * conv[CONV - 1 - s : CONV - s, cols]
    return total


def two(array, c):
    piece = array[c * CHUNK : (c + 1) * CHUNK]
    return jnp.concatenate([piece, piece], axis=0)


def pair(first, second, c):
    at = slice(c * CHUNK, (c + 1) * CHUNK)
    return jnp.concatenate([first[at], second[at]], axis=0)


def unit_rows(v):
    scale = lax.rsqrt(jnp.sum(v * v, axis=-1, keepdims=True) + EPS)
    return v * scale, scale


def token_masks():
    row, col = iota((SPAN, SPAN), 0), iota((SPAN, SPAN), 1)
    tok_r, tok_c = row % CHUNK, col % CHUNK
    strict = (tok_c < tok_r) | ((tok_c == tok_r) & (row >= CHUNK) & (col < CHUNK))
    return tok_r ^ tok_c, strict


def gate_tiles(logits, alpha):
    gates = alpha * softplus(logits)
    sums = mm(chunk_sum_matrix(False), gates, NN, 6)
    flat = jnp.transpose(sums)[:8]
    turned = pltpu.roll(flat, CHUNK, 1)
    lane = iota(flat.shape, 1)
    first = jnp.where(lane < CHUNK, flat, turned)
    second = jnp.where(lane < CHUNK, turned, flat)
    return gates, sums, (first, second)


def spread_column(tile, col):
    return jnp.broadcast_to(tile[:, col : col + 1], (SPAN, DK))


def chunk_gates(span_start, marks, ends, sums, rows, h, c):
    start = span_start + c * CHUNK
    col_place = start + iota((CHUNK, SPAN), 0)
    row_place = start + iota((CHUNK, SPAN), 1) % CHUNK
    col_doc = doc_of(col_place, marks, ends)
    row_doc = doc_of(row_place, marks, ends)
    total = spread_column(sums, 3 * h + 2)[c * CHUNK : (c + 1) * CHUNK]
    across = rows[c][3 * h + 2 : 3 * h + 3]
    kept = (col_doc == row_doc) & (row_place <= col_place)
    decay = jnp.exp(jnp.where(kept, total - across, -1e30))
    doc_before = doc_scalar(start - 1, marks, ends)
    doc_last = doc_scalar(start + CHUNK - 1, marks, ends)
    last = total[CHUNK - 1 : CHUNK]
    opening = jnp.where(col_doc == doc_before, jnp.exp(total), 0.0)
    closing = jnp.where(col_doc == doc_last, jnp.exp(last - total), 0.0)
    whole = jnp.where(doc_before == doc_last, jnp.exp(last), 0.0)
    return decay, opening, closing, whole


def inverses(lowers, apart):
    eye = jnp.where(iota((SPAN, SPAN), 0) == iota((SPAN, SPAN), 1), 1.0, 0.0)
    result = [eye - jnp.where(apart == 0, lower, 0.0) for lower in lowers]
    for level in range(LEVELS):
        here = (apart >> level) == 1
        steps = [
            mm(inverse, jnp.where(here, lower, 0.0), NN, P_INV)
            for inverse, lower in zip(result, lowers)
        ]
        result = [
            inverse - mm(step, inverse, NN, P_INV) for inverse, step in zip(result, steps)
        ]
    return result


def rms_scale(values):
    return lax.rsqrt(jnp.mean(values * values, axis=-1, keepdims=True) + EPS)


def mixer_kernel(
    heads, ends, marks, x, x_halo, gain, w_mixer, w_rates, bias, alpha, conv,
    h_out, raw_out, rim_out, gate_out, logit_out, inv_out, map_out, state_out,
    read_out, own_out, far_out, end_out, ext, state,
):
    step = pl.program_id(0)
    span_start = marks[0] + step * SPAN

    def rounded_norm(rows):
        values = rows.astype(F32)
        return (values * rms_scale(values) * gain[...]).astype(BF16)

    @pl.when(step == 0)
    def _():
        halo = jnp.dot(rounded_norm(x_halo[...]), w_mixer[...], preferred_element_type=F32)
        for h in range(heads):
            ext[0:8, h * QKV : (h + 1) * QKV] = halo[HALO - 8 :, h * MIXW : h * MIXW + QKV]
        rim_out[...] = ext[0:8]
        for h in range(heads):
            state[h, :, :DV] = jnp.zeros((DK, DV), F32)
            state[h, :, DV:] = jnp.where(
                iota((DK, DK), 0) == iota((DK, DK), 1), 1.0, 0.0
            ).astype(F32)

    @pl.when(step > 0)
    def _():
        ext[0:8] = ext[SPAN : SPAN + 8]

    h_one = rounded_norm(x[...])
    h_out[...] = h_one
    raw = jnp.dot(h_one, w_mixer[...], preferred_element_type=F32)
    for h in range(heads):
        ext[8 : 8 + SPAN, h * QKV : (h + 1) * QKV] = raw[:, h * MIXW : h * MIXW + QKV]
        gate_out[:, h * DV : (h + 1) * DV] = raw[:, h * MIXW + QKV : (h + 1) * MIXW]
    raw_out[...] = ext[8 : 8 + SPAN]
    logits = jnp.dot(h_one, w_rates[...], preferred_element_type=F32) + bias[...]
    logit_out[...] = logits
    masks = conv_masks(span_start, marks, ends, SPAN, -1)
    apart, strict = token_masks()
    betas = jax.nn.sigmoid(logits)
    _, sums, rows = gate_tiles(logits, alpha[...])

    units = [(h, c) for h in range(heads) for c in range(SPAN // CHUNK)]
    parts = {}
    for h in range(heads):
        active = []
        for part in range(5):
            mixed = convolved(ext, conv, masks, h, part)
            active.append(mixed * jax.nn.sigmoid(mixed))
        unit = [unit_rows(active[part])[0] for part in range(3)]
        beta = [spread_column(betas, 3 * h + i) for i in range(NH)]
        parts[h] = (unit, active[3:], beta)

    lowers, reads, sides, lasts, wholes, queries = [], [], [], [], [], []
    for h, c in units:
        (query, key_a, key_b), (value_a, value_b), (beta_a, beta_b) = parts[h]
        keys, values, beta = (
            pair(key_a, key_b, c),
            pair(value_a, value_b, c),
            pair(beta_a, beta_b, c),
        )
        query_c = query[c * CHUNK : (c + 1) * CHUNK]
        decay, opening, closing, whole = chunk_gates(
            span_start, marks, ends, sums, rows, h, c
        )
        decay_two = jnp.concatenate([decay, decay], axis=0)
        opening_two = jnp.concatenate([opening, opening], axis=0)
        closing_two = jnp.concatenate([closing, closing], axis=0)
        lowers.append(
            jnp.where(strict, beta * decay_two * mm(keys, keys, NT, P_FWD), 0.0)
        )
        reads.append(decay * mm(query_c, keys, NT, P_FWD))
        sides.append(
            jnp.concatenate([beta * values, beta * opening_two * keys], axis=1)
        )
        lasts.append(closing_two * keys)
        wholes.append(whole)
        queries.append(opening * query_c)
    solved = inverses(lowers, apart)
    pieces = [mm(inverse, side, NN, P_FWD) for inverse, side in zip(solved, sides)]
    maps = [mm(last, piece, TN, P_FWD) for last, piece in zip(lasts, pieces)]
    seen = [mm(read, piece, NN, P_FWD) for read, piece in zip(reads, pieces)]
    diagonal = iota((DK, DK), 0) == iota((DK, DK), 1)
    for index, (h, c) in enumerate(units):
        inv_out[c, h] = solved[index]
        transfer = jnp.where(diagonal, wholes[index], 0.0) - maps[index][:, DV:]
        map_out[c, h] = transfer
        reader = queries[index] - seen[index][:, DV:]
        at, col = slice(c * CHUNK, (c + 1) * CHUNK), slice(h * DK, (h + 1) * DK)
        read_out[at, col] = reader
        before = state[h]
        state_out[c, h] = before
        both = mm(reader, before, NN, P_STATE)
        own_out[at, col] = seen[index][:, :DV] + both[:, :DV]
        far_out[at, col] = both[:, DV:]
        after = mm(transfer, before, NN, P_STATE)
        state[h, :, :DV] = after[:, :DV] + maps[index][:, :DV]
        state[h, :, DV:] = after[:, DV:]
    end_out[...] = state[...]


def block(shape, index):
    return pl.BlockSpec(shape, index)


def fixed(shape):
    return pl.BlockSpec(shape, lambda i: (0,) * len(shape))


SCALARS = pl.BlockSpec(memory_space=pltpu.SMEM)


def shape(dims, kind=F32):
    return jax.ShapeDtypeStruct(dims, kind)


def params(megabytes):
    return pltpu.CompilerParams(
        dimension_semantics=("arbitrary",), vmem_limit_bytes=megabytes << 20
    )


def mixer_forward(heads, ends, marks, x_all, rows, gain, w_mixer, w_rates, bias, alpha, conv):
    model = x_all.shape[1]
    steps, chunks, per = rows // SPAN, rows // CHUNK, SPAN // CHUNK
    wide = heads * QKV
    row = lambda width: block((SPAN, width), lambda i: (i, 0))
    cube = lambda last: block((per, heads, SPAN, last), lambda i: (i, 0, 0, 0))
    return pl.pallas_call(
        functools.partial(mixer_kernel, heads, ends),
        grid=(steps,),
        in_specs=[
            SCALARS,
            row(model),
            block((HALO, model), lambda i: (rows // HALO, 0)),
            fixed((1, model)),
            fixed(w_mixer.shape),
            fixed(w_rates.shape),
            fixed(bias.shape),
            fixed(alpha.shape),
            fixed(conv.shape),
        ],
        out_specs=[
            row(model),
            row(wide),
            fixed((8, wide)),
            row(heads * DV),
            row(DK),
            cube(SPAN),
            cube(DK),
            cube(DK + DV),
            row(heads * DK),
            row(heads * DV),
            row(heads * DK),
            fixed((heads, DK, DK + DV)),
        ],
        out_shape=[
            shape((rows, model), BF16),
            shape((rows, wide)),
            shape((8, wide)),
            shape((rows, heads * DV)),
            shape((rows, DK)),
            shape((chunks, heads, SPAN, SPAN)),
            shape((chunks, heads, DK, DK)),
            shape((chunks, heads, DK, DK + DV)),
            shape((rows, heads * DK)),
            shape((rows, heads * DV)),
            shape((rows, heads * DK)),
            shape((heads, DK, DK + DV)),
        ],
        scratch_shapes=[
            pltpu.VMEM((8 + SPAN, wide), F32),
            pltpu.VMEM((heads, DK, DK + DV), F32),
        ],
        compiler_params=params(40),
        name="mixer_forward",
    )(marks, x_all, x_all, gain, w_mixer, w_rates, bias, alpha, conv)


def branch_kernel(heads, place, maps, own, far, gate, gain, w_out, attn_out, normed_out, branch_out, start_out, start):
    @pl.when(pl.program_id(0) == 0)
    def _():
        start[...] = jnp.zeros_like(start)

        def join(j, carry):
            for h in range(heads):
                start[h] = (
                    mm(maps[j, h, :, DV:].astype(F32), start[h], NN, P_STATE)
                    + maps[j, h, :, :DV].astype(F32)
                )
            return carry

        lax.fori_loop(0, place[0], join, 0)
        start_out[...] = start[...]

    for h in range(heads):
        col = slice(h * DV, (h + 1) * DV)
        attn = own[:, col] + mm(far[:, col], start[h], NN, P_STATE)
        attn_out[:, col] = attn
        gates = gate[:, col]
        normed = attn * rms_scale(attn) * gain[...] * (gates * jax.nn.sigmoid(gates))
        normed_out[:, col] = normed.astype(BF16)
    branch_out[...] = jnp.dot(
        normed_out[...], w_out[...], preferred_element_type=F32
    ).astype(BF16)


def branch_forward(heads, place, maps, own, far, gate, gain, w_out):
    rows, model = own.shape[0], w_out.shape[1]
    wide = heads * DV
    row = lambda width: block((ROWS, width), lambda i: (i, 0))
    return pl.pallas_call(
        functools.partial(branch_kernel, heads),
        grid=(rows // ROWS,),
        in_specs=[
            SCALARS, fixed(maps.shape), row(wide), row(wide), row(wide), fixed(gain.shape), fixed(w_out.shape),
        ],
        out_specs=[row(wide), row(wide), row(model), fixed((heads, DK, DV))],
        out_shape=[
            shape((rows, wide)),
            shape((rows, wide), BF16),
            shape((rows, model), BF16),
            shape((heads, DK, DV)),
        ],
        scratch_shapes=[pltpu.VMEM((heads, DK, DV), F32)],
        compiler_params=params(32),
        name="branch_forward",
    )(place, maps, own, far, gate, gain, w_out)


def ffn_kernel(x, branch, grad, gain, w_gate, w_up, w_down, h_out, act_out, gg_out, gu_out, part_out, dh_out):
    resid = x[...].astype(F32) + branch[...].astype(F32)
    h_two = (resid * rms_scale(resid) * gain[...]).astype(BF16)
    h_out[...] = h_two
    gate = mm(h_two, w_gate[...])
    up = mm(h_two, w_up[...])
    sig = jax.nn.sigmoid(gate)
    silu = gate * sig
    act = (silu * up).astype(BF16)
    act_out[...] = act
    grad_act = mm(grad[...], w_down[...], NT)
    grad_gate = (grad_act * up * sig * (1.0 + gate * (1.0 - sig))).astype(BF16)
    grad_up = (grad_act * silu).astype(BF16)
    gg_out[...] = grad_gate
    gu_out[...] = grad_up
    dh_out[...] = (mm(grad_gate, w_gate[...], NT) + mm(grad_up, w_up[...], NT)).astype(BF16)
    part_out[...] = mm(act, w_down[...]).astype(BF16)


def ffn_pass(x_all, branch, grad, gain, w_gate, w_up, w_down):
    rows, model = branch.shape
    hidden = w_gate.shape[1]
    row = lambda width: block((ROWS, width), lambda i: (i, 0))
    return pl.pallas_call(
        ffn_kernel,
        grid=(rows // ROWS,),
        in_specs=[
            row(model), row(model), row(model), fixed(gain.shape), fixed(w_gate.shape), fixed(w_up.shape), fixed(w_down.shape),
        ],
        out_specs=[row(model), row(hidden), row(hidden), row(hidden), row(model), row(model)],
        out_shape=[
            shape((rows, model), BF16),
            shape((rows, hidden), BF16),
            shape((rows, hidden), BF16),
            shape((rows, hidden), BF16),
            shape((rows, model), BF16),
            shape((rows, model), BF16),
        ],
        compiler_params=params(48),
        name="ffn_pass",
    )(x_all, branch, grad, gain, w_gate, w_up, w_down)


def fold(value):
    return jnp.sum(value.reshape(value.shape[0] // 8, 8, value.shape[1]), axis=0)


def resid_kernel(
    heads, x, branch, dh, grad, gain, w_out, attn, gate, out_gain, far,
    resid_out, branch_grad_out, attn_grad_out, gate_grad_out, gain_grad_out, out_gain_grad_out, state_grad_out,
):
    @pl.when(pl.program_id(0) == 0)
    def _():
        gain_grad_out[...] = jnp.zeros_like(gain_grad_out)
        out_gain_grad_out[...] = jnp.zeros_like(out_gain_grad_out)
        state_grad_out[...] = jnp.zeros_like(state_grad_out)

    resid = x[...].astype(F32) + branch[...].astype(F32)
    scale = rms_scale(resid)
    unit = resid * scale
    grad_h = dh[...].astype(F32)
    gain_grad_out[...] += fold(grad_h * unit)
    lifted = grad_h * gain[...]
    grad_resid = grad[...].astype(F32) + scale * (
        lifted - unit * jnp.mean(lifted * unit, axis=-1, keepdims=True)
    )
    resid_out[...] = grad_resid
    grad_branch = grad_resid.astype(BF16)
    branch_grad_out[...] = grad_branch
    grad_normed = mm(grad_branch, w_out[...], NT)
    for h in range(heads):
        col = slice(h * DV, (h + 1) * DV)
        value, gates, back = attn[:, col], gate[:, col], grad_normed[:, col]
        scale_o = rms_scale(value)
        unit_o = value * scale_o
        sig = jax.nn.sigmoid(gates)
        silu = gates * sig
        gate_grad_out[:, col] = (
            back * unit_o * out_gain[...] * sig * (1.0 + gates * (1.0 - sig))
        ).astype(BF16)
        scaled = back * silu
        out_gain_grad_out[...] += fold(scaled * unit_o)
        lifted_o = scaled * out_gain[...]
        grad_attn = scale_o * (
            lifted_o - unit_o * jnp.mean(lifted_o * unit_o, axis=-1, keepdims=True)
        )
        attn_grad_out[:, col] = grad_attn
        state_grad_out[h] += mm(far[:, col], grad_attn, TN, P_STATE)


def resid_backward(heads, x_all, branch, dh, grad, gain, w_out, attn, gate, out_gain, far):
    rows, model = branch.shape
    wide = heads * DV
    row = lambda width: block((ROWS, width), lambda i: (i, 0))
    return pl.pallas_call(
        functools.partial(resid_kernel, heads),
        grid=(rows // ROWS,),
        in_specs=[
            row(model), row(model), row(model), row(model), fixed(gain.shape), fixed(w_out.shape),
            row(wide), row(wide), fixed(out_gain.shape), row(wide),
        ],
        out_specs=[
            row(model), row(model), row(wide), row(wide),
            fixed((8, model)), fixed((8, DV)), fixed((heads, DK, DV)),
        ],
        out_shape=[
            shape((rows, model)),
            shape((rows, model), BF16),
            shape((rows, wide)),
            shape((rows, wide), BF16),
            shape((8, model)),
            shape((8, DV)),
            shape((heads, DK, DV)),
        ],
        compiler_params=params(48),
        name="resid_backward",
    )(x_all, branch, dh, grad, gain, w_out, attn, gate, out_gain, far)


def mixer_back_kernel(
    heads, ends, steps, marks, place, maps, state_grads, start, raw, raw_before, rim, conv, logits, alpha,
    inv, transfers, states, end_state, reads, attn_grad, gate_grad,
    grad_raw_out, tail_out, rim_out, rates_out, sums_out, conv_out,
    ext, mixed_grad, carry, after,
):
    step = pl.program_id(0)
    at_step = steps - 1 - step
    span_start = marks[0] + at_step * SPAN
    wide = heads * QKV
    per = SPAN // CHUNK

    @pl.when(step == 0)
    def _():
        carry[...] = jnp.zeros_like(carry)
        count = maps.shape[0]

        def join(k, unused):
            j = count - 1 - k
            for h in range(heads):
                carry[h] = (
                    mm(maps[j, h, :, DV:].astype(F32), carry[h], TN, P_STATE)
                    + state_grads[j, h].astype(F32)
                )
            return unused

        lax.fori_loop(0, count - 1 - place[0], join, 0)
        for h in range(heads):
            after[h] = end_state[h, :, :DV] + mm(
                end_state[h, :, DV:], start[h], NN, P_STATE
            )
        mixed_grad[0:8] = jnp.zeros((8, wide), F32)
        mixed_grad[8 + SPAN :] = jnp.zeros((8, wide), F32)
        sums_out[...] = jnp.zeros_like(sums_out)
        conv_out[...] = jnp.zeros_like(conv_out)

    @pl.when(step > 0)
    def _():
        mixed_grad[8 + SPAN :] = mixed_grad[8:16]

    @pl.when(at_step == 0)
    def _():
        ext[0:8] = rim[...]

    @pl.when(at_step > 0)
    def _():
        ext[0:8] = raw_before[...]

    ext[8 : 8 + SPAN] = raw[...]
    masks = conv_masks(span_start, marks, ends, SPAN, -1)
    apart, strict = token_masks()
    logit = logits[...]
    betas = jax.nn.sigmoid(logit)
    gates, sums, rows = gate_tiles(logit, alpha[...])

    parts = {}
    for h in range(heads):
        mixed = [convolved(ext, conv, masks, h, part) for part in range(5)]
        active = [m * jax.nn.sigmoid(m) for m in mixed]
        unit, scale = zip(*[unit_rows(active[part]) for part in range(3)])
        beta = [spread_column(betas, 3 * h + i) for i in range(NH)]
        parts[h] = (mixed, unit, scale, active[3:], beta)

    units = [(h, c) for h in range(heads) for c in range(per)]
    befores, grads_after, befores_next = {}, {}, {}
    for h in range(heads):
        for c in reversed(range(per)):
            at, col = slice(c * CHUNK, (c + 1) * CHUNK), slice(h * DK, (h + 1) * DK)
            befores[h, c] = states[c, h, :, :DV] + mm(
                states[c, h, :, DV:], start[h], NN, P_STATE
            )
            befores_next[h, c] = after[h] if c == per - 1 else befores[h, c + 1]
        for c in reversed(range(per)):
            at, col = slice(c * CHUNK, (c + 1) * CHUNK), slice(h * DK, (h + 1) * DK)
            grads_after[h, c] = carry[h]
            carry[h] = mm(reads[at, col], attn_grad[at, col], TN, P_STATE) + mm(
                transfers[c, h], carry[h], TN, P_STATE
            )
        after[h] = befores[h, 0]

    work = {}
    for h, c in units:
        _, unit, _, values, beta = parts[h]
        keys = pair(unit[1], unit[2], c)
        value = pair(values[0], values[1], c)
        beta_c = pair(beta[0], beta[1], c)
        query = unit[0][c * CHUNK : (c + 1) * CHUNK]
        decay, opening, closing, _ = chunk_gates(span_start, marks, ends, sums, rows, h, c)
        decay_two = jnp.concatenate([decay, decay], axis=0)
        opening_two = jnp.concatenate([opening, opening], axis=0)
        closing_two = jnp.concatenate([closing, closing], axis=0)
        grown = jnp.where(strict, decay_two * mm(keys, keys, NT, P_BWD), 0.0)
        read = decay * mm(query, keys, NT, P_BWD)
        recalled = opening_two * mm(keys, befores[h, c], NN, P_BWD)
        missing = value - recalled
        deltas = mm(inv[c, h], beta_c * missing, NN, P_BWD)
        at, col = slice(c * CHUNK, (c + 1) * CHUNK), slice(h * DK, (h + 1) * DK)
        out_grad = attn_grad[at, col]
        grad_deltas = mm(read, out_grad, TN, P_BWD) + mm(
            closing_two * keys, grads_after[h, c], NN, P_BWD
        )
        work[h, c] = [
            keys, query, beta_c, decay, decay_two, opening, opening_two, closing_two,
            grown, missing, deltas, out_grad, grad_deltas,
        ]
    columns = {}
    for h, c in units:
        (
            keys, query, beta, decay, decay_two, opening, opening_two, closing_two,
            grown, missing, deltas, out_grad, grad_deltas,
        ) = work[h, c]
        grad_target = mm(inv[c, h], grad_deltas, TN, P_BWD)
        grad_lower = jnp.where(strict, -mm(grad_target, deltas, NT, P_BWD), 0.0)
        grad_beta = jnp.sum(grad_lower * grown, axis=-1, keepdims=True) + jnp.sum(
            grad_target * missing, axis=-1, keepdims=True
        )
        grad_pairs = grad_lower * beta * decay_two
        grad_value = beta * grad_target
        grad_read = decay * mm(out_grad, deltas, NT, P_BWD)
        left = mm(grad_pairs, keys, NN, P_BWD) - beta * opening_two * mm(
            grad_target, befores[h, c], NT, P_BWD
        )
        right = (
            mm(grad_pairs, keys, TN, P_BWD)
            + closing_two * mm(deltas, grads_after[h, c], NT, P_BWD)
            + mm(grad_read, query, TN, P_BWD)
        )
        grad_query = mm(grad_read, keys, NN, P_BWD) + opening * mm(
            out_grad, befores[h, c], NT, P_BWD
        )
        in_left = jnp.sum(keys * left, axis=-1, keepdims=True)
        in_right = jnp.sum(keys * right, axis=-1, keepdims=True)
        in_query = jnp.sum(query * grad_query, axis=-1, keepdims=True)
        spare = in_left - in_right
        grad_total = spare[:CHUNK] + spare[CHUNK:] + in_query
        whole = jnp.sum(grads_after[h, c] * befores_next[h, c])
        last_row = iota((CHUNK, 1), 0) == CHUNK - 1
        grad_total = grad_total + jnp.where(last_row, whole, 0.0)
        columns[h, c] = (
            grad_query - query * in_query,
            left + right - keys * (in_left + in_right),
            grad_value,
            grad_beta,
            grad_total,
        )

    lane = iota((SPAN, DK), 1)
    rates = jnp.zeros((SPAN, DK), F32)
    for h in range(heads):
        mixed, unit, scale, values, beta = parts[h]
        got = [columns[h, c] for c in range(per)]
        low, high = slice(0, CHUNK), slice(CHUNK, 2 * CHUNK)
        stack = lambda index, part: jnp.concatenate([g[index][part] for g in got], axis=0)
        act_grads = [
            scale[0] * stack(0, low),
            scale[1] * stack(1, low),
            scale[2] * stack(1, high),
            stack(2, low),
            stack(2, high),
        ]
        for i, column in enumerate((stack(3, low), stack(3, high), stack(4, low))):
            rates = rates + jnp.where(lane == 3 * h + i, column, 0.0)
        for part in range(5):
            cols = part_columns(h, part)
            sig = jax.nn.sigmoid(mixed[part])
            grad = act_grads[part] * sig * (1.0 + mixed[part] * (1.0 - sig))
            mixed_grad[8 : 8 + SPAN, cols] = grad
            conv_out[24:32, cols] += fold(grad * ext[8 : 8 + SPAN, cols])
            for s in range(1, CONV):
                moved = jnp.where(masks[s], ext[8 - s : 8 - s + SPAN, cols], 0.0)
                tap = CONV - 1 - s
                conv_out[8 * tap : 8 * tap + 8, cols] += fold(grad * moved)

    ahead = conv_masks(span_start, marks, ends, SPAN, 1)
    for h in range(heads):
        for part in range(5):
            cols = part_columns(h, part)
            grad = mixed_grad[8 : 8 + SPAN, cols] * conv[CONV - 1 : CONV, cols]
            for s in range(1, CONV):
                moved = jnp.where(ahead[s], mixed_grad[8 + s : 8 + s + SPAN, cols], 0.0)
                grad = grad + moved * conv[CONV - 1 - s : CONV - s, cols]
            begin = h * MIXW + part * DK
            grad_raw_out[:, begin : begin + DK] = grad.astype(BF16)

            @pl.when(step == 0)
            def _():
                tail_out[:, cols] = grad[SPAN - HALO :]

        grad_raw_out[:, h * MIXW + QKV : (h + 1) * MIXW] = gate_grad[:, h * DV : (h + 1) * DV]

    @pl.when(at_step == 0)
    def _():
        rim_masks = conv_masks(marks[0] - 8, marks, ends, 8, 1)
        for h in range(heads):
            for part in range(5):
                cols = part_columns(h, part)
                grad = jnp.zeros((8, DK), F32)
                for s in range(1, CONV):
                    moved = jnp.where(rim_masks[s], mixed_grad[s : s + 8, cols], 0.0)
                    grad = grad + moved * conv[CONV - 1 - s : CONV - s, cols]
                rim_out[:, cols] = grad

    back = mm(chunk_sum_matrix(True), rates, NN, 6)
    lanes = iota((1, DK), 1)
    is_gate = (lanes % (NH + 1) == NH) & (lanes < heads * (NH + 1))
    grad_logits = jnp.where(is_gate, back * alpha[...] * betas, rates * betas * (1.0 - betas))
    rates_out[...] = grad_logits.astype(BF16)
    sums_out[0:8] += fold(grad_logits)
    sums_out[8:16] += fold(back * gates)


def mixer_backward(
    heads, ends, marks, place, maps, state_grads, start, raw, rim, conv, logits, alpha,
    inv, transfers, states, end_state, reads, attn_grad, gate_grad,
):
    rows, wide = raw.shape
    steps, per = rows // SPAN, SPAN // CHUNK
    turn = lambda i: steps - 1 - i
    row = lambda width: block((SPAN, width), lambda i: (turn(i), 0))
    cube = lambda last: block((per, heads, SPAN, last), lambda i: (turn(i), 0, 0, 0))
    return pl.pallas_call(
        functools.partial(mixer_back_kernel, heads, ends, steps),
        grid=(steps,),
        in_specs=[
            SCALARS,
            SCALARS,
            fixed(maps.shape),
            fixed(state_grads.shape),
            fixed(start.shape),
            row(wide),
            block((8, wide), lambda i: (jnp.maximum(turn(i) * (SPAN // 8) - 1, 0), 0)),
            fixed(rim.shape),
            fixed(conv.shape),
            row(DK),
            fixed(alpha.shape),
            cube(SPAN),
            cube(DK),
            cube(DK + DV),
            fixed(end_state.shape),
            row(heads * DK),
            row(heads * DV),
            row(heads * DV),
        ],
        out_specs=[
            row(heads * MIXW),
            fixed((HALO, wide)),
            fixed((8, wide)),
            row(DK),
            fixed((16, DK)),
            fixed((8 * CONV, wide)),
        ],
        out_shape=[
            shape((rows, heads * MIXW), BF16),
            shape((HALO, wide)),
            shape((8, wide)),
            shape((rows, DK), BF16),
            shape((16, DK)),
            shape((8 * CONV, wide)),
        ],
        scratch_shapes=[
            pltpu.VMEM((8 + SPAN, wide), F32),
            pltpu.VMEM((8 + SPAN + 8, wide), F32),
            pltpu.VMEM((heads, DK, DV), F32),
            pltpu.VMEM((heads, DK, DV), F32),
        ],
        compiler_params=params(48),
        name="mixer_backward",
    )(
        marks, place, maps, state_grads, start, raw, raw, rim, conv, logits, alpha,
        inv, transfers, states, end_state, reads, attn_grad, gate_grad,
    )


def shifted(value, axis, steps):
    count = lax.axis_size(axis)
    first, last = (max(0, -steps), min(count, count - steps))
    return lax.ppermute(value, axis, [(source, source + steps) for source in range(first, last)])


def dot_t(leading, trailing):
    return lax.dot_general(leading, trailing, NT, preferred_element_type=F32)


def t_dot(leading, trailing):
    return lax.dot_general(leading, trailing, TN, preferred_element_type=F32)


def norm_back(grad_unit, unit, inv_scale):
    return inv_scale * (grad_unit - unit * jnp.mean(grad_unit * unit, axis=-1, keepdims=True))


def local(
    tokens, lengths, norm1_gain, w_mixer, w_rates, decay_log, rates_bias, conv_weight,
    out_gain, w_out, norm2_gain, w_ffn_gate, w_ffn_up, w_ffn_down, out_grad,
):
    rows, share = tokens.shape
    heads = decay_log.shape[0]
    ends = lengths.shape[0]
    place = lax.axis_index("seq")
    col_start = lax.axis_index("head") * share
    marks = jnp.concatenate(
        [jnp.reshape(place * rows, (1,)), jnp.cumsum(lengths)]
    ).astype(jnp.int32)
    place_arg = jnp.reshape(place, (1,)).astype(jnp.int32)

    halo = shifted(tokens[rows - HALO :], "seq", 1)
    x_all = lax.all_gather(
        jnp.concatenate([tokens, halo], axis=0), "head", axis=1, tiled=True
    )
    grad_full = lax.all_gather(out_grad, "head", axis=1, tiled=True)
    gain_one, gain_two = norm1_gain[None, :], norm2_gain[None, :]
    gain_out = out_gain[None, :]
    spare = DK - heads * (NH + 1)
    rates_w = jnp.pad(w_rates, ((0, 0), (0, spare)))
    bias = jnp.pad(rates_bias, (0, spare))[None, :]
    none = jnp.zeros((heads,), F32)
    alpha = jnp.stack([none] * NH + [-jnp.exp(decay_log)], axis=-1).reshape(-1)
    alpha = jnp.pad(alpha, (0, spare))[None, :]

    (
        h_one, raw, rim, gate_o, logits, inv, transfers, states, reads, own, far, end_state,
    ) = mixer_forward(
        heads, ends, marks, x_all, rows, gain_one, w_mixer, rates_w, bias, alpha, conv_weight
    )
    maps = lax.all_gather(end_state.astype(BF16), "seq")
    attn, normed, branch_part, start = branch_forward(
        heads, place_arg, maps, own, far, gate_o, gain_out, w_out
    )
    branch = lax.psum(branch_part, "head")
    h_two, act, grad_gate, grad_up, ffn_part, dh_part = ffn_pass(
        x_all, branch, grad_full, gain_two, w_ffn_gate, w_ffn_up, w_ffn_down
    )
    dh = lax.psum(dh_part, "head")
    ffn_share = lax.psum_scatter(ffn_part, "head", scatter_dimension=1, tiled=True)
    grad_down = t_dot(act, grad_full)
    grad_wgate = t_dot(h_two, grad_gate)
    grad_wup = t_dot(h_two, grad_up)
    own_cols = lambda value: lax.dynamic_slice_in_dim(value, col_start, share, 1)
    resid_own = own_cols(x_all[:rows]).astype(F32) + own_cols(branch).astype(F32)
    output = (resid_own + ffn_share.astype(F32)).astype(BF16)

    (
        grad_resid, grad_branch, grad_attn, grad_gate_o, gain_two_part, out_gain_part, state_grad,
    ) = resid_backward(
        heads, x_all, branch, dh, grad_full, gain_two, w_out, attn, gate_o, gain_out, far
    )
    grad_wout = t_dot(normed, grad_branch)
    state_grads = lax.all_gather(state_grad.astype(BF16), "seq")
    grad_raw, tail, rim_grad, grad_rates, sums, conv_parts = mixer_backward(
        heads, ends, marks, place_arg, maps, state_grads, start, raw, rim, conv_weight, logits, alpha,
        inv, transfers, states, end_state, reads, grad_attn, grad_gate_o,
    )
    rim_back = shifted(rim_grad, "seq", -1)
    tail = tail.at[HALO - 8 :].add(rim_back)
    for h in range(heads):
        grad_raw = lax.dynamic_update_slice(
            grad_raw, tail[:, h * QKV : (h + 1) * QKV].astype(BF16), (rows - HALO, h * MIXW)
        )
    grad_wmixer = t_dot(h_one, grad_raw)
    grad_rates = grad_rates[:, : heads * (NH + 1)]
    grad_wrates = t_dot(h_one, grad_rates)
    grad_h_part = dot_t(grad_raw, w_mixer) + dot_t(grad_rates, w_rates)
    grad_h_one = lax.psum(grad_h_part.astype(BF16), "head").astype(F32)
    x_full = x_all[:rows].astype(F32)
    scale_one = rms_scale(x_full)
    unit_one = x_full * scale_one
    grad_norm1 = jnp.sum(grad_h_one * unit_one, axis=0)
    grad_tokens = grad_resid + norm_back(grad_h_one * norm1_gain, unit_one, scale_one)
    tokens_grad = own_cols(grad_tokens).astype(BF16)

    sum_rows = jnp.sum(sums.reshape(2, 8, DK), axis=1)
    grad_bias = sum_rows[0, : heads * (NH + 1)]
    grad_decay = sum_rows[1, : heads * (NH + 1)].reshape(heads, NH + 1)[:, NH]
    grad_conv = jnp.sum(conv_parts.reshape(CONV, 8, heads * QKV), axis=1)
    grad_outgain = lax.psum(jnp.sum(out_gain_part, axis=0), "head")
    small = lax.psum(
        (grad_norm1, grad_outgain, jnp.sum(gain_two_part, axis=0), grad_decay, grad_bias, grad_conv),
        "seq",
    )
    scatter = lambda value, axis: lax.psum_scatter(
        value.astype(BF16), "seq", scatter_dimension=axis, tiled=True
    ).astype(F32)
    return (
        output, tokens_grad, small[0], scatter(grad_wmixer, 0), scatter(grad_wrates, 0),
        small[3], small[4], small[5], small[1], scatter(grad_wout, 1), small[2],
        scatter(grad_wgate, 0), scatter(grad_wup, 0), scatter(grad_down, 1),
    )


def solution(mesh):
    placed = (
        P("seq", "head"), P(), P(), P(None, "head"), P(None, "head"), P("head"), P("head"), P(None, "head"),
        P(), P("head", None), P(), P(None, "head"), P(None, "head"), P("head", None), P("seq", "head"),
    )
    return jax.shard_map(
        local,
        mesh=mesh,
        in_specs=placed,
        out_specs=(
            P("seq", "head"), P("seq", "head"), P(), P("seq", "head"), P("seq", "head"), P("head"), P("head"),
            P(None, "head"), P(), P("head", "seq"), P(), P("seq", "head"), P("seq", "head"), P("head", "seq"),
        ),
        check_vma=False,
    )
```

time: 4050 us -> 883 us (0.22); the launches traced: 3990 us -> 881 us
  other arithmetic: 1530 us -> 20.9 us
  matrix products: 1250 us -> 33.4 us
  local copies, waits for them, and re-layouts: 574 us -> 46.7 us
  Pallas kernels: 0 us -> 122 us
  waiting for transfers between devices: 491 us -> 562 us
    another operation x533 -> x3, other arithmetic: 1110 us -> 1.5 us  [the longest x384 1040 us: advance(): jax.scipy.linalg.solve_triangular(system, right_side, lower=True, unit_di...]
    dot_general x803 -> x8, matrix products: 1120 us -> 33.4 us  [the longest x6 25.1 us: t_dot(): return lax.dot_general(leading, trailing, TN, preferred_element_type=F32)]
    dynamic_update_slice x224 -> x2, local copies, waits for them, and re-layouts: 191 us -> 1.2 us  [local(): lax.dynamic_update_slice(grad_raw, tail[:, h * QKV:(h + 1) * QKV].astype(...]
    another operation x128 -> x0, matrix products: 127 us -> none  [advance(): jax.scipy.linalg.solve_triangular(system, right_side, lower=True, unit_di...]
    pallas_call x0 -> x5, Pallas kernels: none -> 122 us  [the longest x1 52.8 us: mixer_backward(): pl.pallas_call(functools.partial(mixer_back_kernel, heads, ends, steps),...]
    reduce_sum x108 -> x5, other arithmetic: 112 us -> 0.58 us  [the longest x1 0.48 us: rms_scale(): return lax.rsqrt(jnp.mean(values * values, axis=-1, keepdims=True) + EPS)]
    dynamic_update_slice x96 -> x0, other arithmetic: 107 us -> none  [group_pass(): lax.scan(advance, state, (split(query_sub), split(key_sub), split(value_s...]
    psum x3, waiting for transfers between devices: 65.5 us -> 156 us  [the longest x1 53.6 us: local(): branch = lax.psum(branch_part, 'head')]
  transfers between devices with their start and end apart: 16 -> 15, of which waited for: 12 -> 14; matrix products, arithmetic and copies ran while one was open for 32% -> 8% of each run, Pallas kernels for 0% -> 0%
where the time goes in v1:
time: 883 us; the launch traced here: 881 us
  waiting for transfers between devices  562 us (64%)
  Pallas kernels  122 us (14%)
  blocking collectives  75.6 us (9%)
  local copies, waits for them, and re-layouts  46.7 us (5%)
  matrix products  33.4 us (4%)
  other arithmetic  20.9 us (2%)
  between operations  14.2 us (2%)
    unnamed x18, waiting for transfers between devices  225 us
    reduce_scatter x1, waiting for transfers between devices, local(): lax.psum_scatter(value.astype(BF16), 'seq', scatter_dimension=axis, tiled...  75.7 us
    psum x1, waiting for transfers between devices, local(): branch = lax.psum(branch_part, 'head')  53.6 us
    pallas_call x1, Pallas kernels, mixer_backward(): pl.pallas_call(functools.partial(mixer_back_kernel, heads, ends, steps),...  52.8 us
    psum x1, waiting for transfers between devices, local(): dh = lax.psum(dh_part, 'head')  51.6 us
    psum x1, waiting for transfers between devices, local(): grad_h_one = lax.psum(grad_h_part.astype(BF16), 'head').astype(F32)  51.3 us
    unnamed x86, local copies, waits for them, and re-layouts  44.3 us
    pallas_call x1, Pallas kernels, mixer_forward(): pl.pallas_call(functools.partial(mixer_kernel, heads, ends), grid=(steps,...  41.7 us
  transfers between devices with their start and end apart: 15, of which 14 were waited for; matrix products, arithmetic and copies ran while one was open for 8% of the time, Pallas kernels for 0%

profile of v1, /device:TPU:0, one launch (start us, length us, event | category | flops | bytes accessed | tf_op | source)
XLA Modules:
  0.0 881.3 jit_solution(6550233927753772461)
XLA Ops:
  8.0 4.8 collective-permute-start
  19.0 22.4 %all-gather.6.cloned.1.call-done.x.x_halo = bf16[1040,1024]{1,0:T(8,128)(2,1)} async-done(((bf16[1040,256]{1,0:T(8,128)(2,1)}), bf16[1040,1024]{1,0:T(8,128)(2,1)}) %all-gather.6.cloned.1.call-update) | async-done | bytes 2129936 | tf_op jit(solution)/shard_map/all_gather | solution.py:838
  42.9 41.7 %mixer_forward.1 = (bf16[1024,1024]{1,0:T(8,128)(2,1)S(1)}, f32[1024,1280]{1,0:T(8,128)}, f32[8,1280]{1,0:T(8,128)S(1)}, f32[1024,256]{1,0:T(8,128)S(1)}, f32[10...) custom-call(s32[4]{0:T(128)S(1)} %pad_add_fusion.marks, ...), custom_call_target="tpu_custom_call" | custom-call | tf_op jit(solution)/shard_map/mixer_forward/pallas_call | solution.py:311
  93.5 39.5 %all-gather.10.cloned.1.call-done = bf16[16,128,256]{2,1,0:T(8,128)(2,1)} async-done(((bf16[2,128,256]{2,1,0:T(8,128)(2,1)}), bf16[16,128,256]{2,1,0:T(8,128)(2,1)}) %all-gather.10.cloned.1.call-update) | async-done | bytes 1048592 | tf_op jit(solution)/shard_map/all_gather | solution.py:856
  140.4 2.7 copy.39.w_gate
  143.1 2.6 copy.40.w_up
  145.7 10.5 %all-gather.8.cloned.1.call-done.grad = bf16[1024,1024]{1,0:T(8,128)(2,1)} async-done(((bf16[1024,256]{1,0:T(8,128)(2,1)}), bf16[1024,1024]{1,0:T(8,128)(2,1)}) %all-gather.8.cloned.1.call-update) | async-done | bytes 2097168 | tf_op jit(solution)/shard_map/all_gather | solution.py:841
  156.3 53.6 %all-reduce.9.cloned.1.call-done.branch = bf16[1024,1024]{1,0:T(8,128)(2,1)} async-done(((bf16[1024,1024]{1,0:T(8,128)(2,1)}), bf16[1024,1024]{1,0:T(8,128)(2,1)}) %all-reduce.9.cloned.1.call-update) | async-done | bytes 2097168 | tf_op jit(solution)/shard_map/psum | solution.py:860
  211.3 16.4 %ffn_pass.1 = (bf16[1024,1024]{1,0:T(8,128)(2,1)}, bf16[1024,704]{1,0:T(8,128)(2,1)S(1)}, bf16[1024,704]{1,0:T(8,128)(2,1)S(1)}, bf16[1024,704]{1,0:T(8,128)(2,1...) custom-call(bf16[1040,1024]{1,0:T(8,128)(2,1)} %all-gather.6.cloned.1.call-done.x.x_halo, ...), custom_call_target="tpu_custom_call" | custom-call | tf_op jit(solution)/shard_map/ffn_pass/pallas_call | solution.py:436
  231.2 51.6 %all-reduce.11.cloned.1.call-done.dh = bf16[1024,1024]{1,0:T(8,128)(2,1)} async-done(((bf16[1024,1024]{1,0:T(8,128)(2,1)}), bf16[1024,1024]{1,0:T(8,128)(2,1)}) %all-reduce.11.cloned.1.call-update) | async-done | bytes 2097168 | tf_op jit(solution)/shard_map/psum | solution.py:864
  284.7 8.8 resid_backward.1
  293.5 31.6 %all-gather.1 = bf16[16,128,128]{2,1,0:T(8,128)(2,1)S(1)} all-gather(bf16[2,128,128]{2,1,0:T(8,128)(2,1)S(1)} %convert_element_type.79), channel_id=3, replica_groups=mesh['seq'=8,'head'=4] {'seq'}, dimensions={0}, use_global_device_ids=true | all-gather | bytes 589824 | tf_op jit(solution)/shard_map/all_gather | solution.py:879
  325.1 52.8 %mixer_backward.1 = (bf16[1024,1536]{1,0:T(8,128)(2,1)}, f32[16,1280]{1,0:T(8,128)S(1)}, f32[8,1280]{1,0:T(8,128)}, bf16[1024,128]{1,0:T(8,128)(2,1)S(1)}, f32[1...) custom-call(s32[4]{0:T(128)S(1)} %copy-done.28, s32[1]{0:T(128)} %bitcast.place, bf16[8,2,128,256]{3,2,1,0:T(8,128)(2,1)S(1)} %bitcast.43, ...), custom_call_target="tpu_custom_call" | custom-call | tf_op jit(solution)/shard_map/mixer_backward/pallas_call | solution.py:752
  380.5 3.1 convolution_convert_fusion.4
  387.0 6.3 fusion.6
  395.4 4.9 convolution_convert_fusion.3
  403.2 4.9 convolution_convert_fusion.2
  410.7 4.9 convolution_convert_fusion.1
  415.7 2.6 copy.49
  418.9 6.7 convolution_convert_fusion
  428.1 6.1 psum.77
  434.4 6.7 reduce-scatter.22.cloned.1.call-done
  442.5 63.4 %reduce-scatter.24.cloned.1.call-done = bf16[128,256]{1,0:T(8,128)(2,1)} async-done(((bf16[1024,256]{1,0:T(8,128)(2,1)}), bf16[128,256]{1,0:T(8,128)(2,1)}) %reduce-scatter.24.cloned.1.call-update) | async-done | bytes 65552
  507.6 51.3 %all-reduce.13.cloned.1.call-done = bf16[1024,1024]{1,0:T(8,128)(2,1)} async-done(((bf16[1024,1024]{1,0:T(8,128)(2,1)}), bf16[1024,1024]{1,0:T(8,128)(2,1)}) %all-reduce.13.cloned.1.call-update) | async-done | bytes 2097168 | tf_op jit(solution)/shard_map/psum | solution.py:894
  558.9 5.4 fusion.1
  564.3 37.9 %all-reduce.4 = (f32[1024]{0:T(1024)}, f32[2]{0:T(128)}, f32[6]{0:T(128)}, f32[4,1280]{1,0:T(4,128)}, f32[128]{0:T(128)}, /*index=5*/f32[1024]{0:T(1024)}) all-reduce(f32[1024]{0:T(1024)S(1)} %get-tuple-element.96, f32[2]{0:T(128)S(1)} %slice_reduce_fusion, f32[6]{0:T(128)S(1)} %get-tuple-element.106, ...), channel_id=1, replica_groups=mesh['seq'=8,'head'=4] {'seq'}, use_global_device_ids=true, to_apply=%region_8.9 | all-reduce | flops 7304 | bytes 58432 | tf_op jit(solution)/shard_map/psum | solution.py:907
  602.2 3.0 fusion.2
  605.2 22.1 %reduce-scatter.26.cloned.1.call-done = bf16[128,704]{1,0:T(8,128)(2,1)} async-done(((bf16[1024,704]{1,0:T(8,128)(2,1)}), bf16[128,704]{1,0:T(8,128)(2,1)}) %reduce-scatter.26.cloned.1.call-update) | async-done | bytes 180240
  629.1 65.6 %reduce-scatter.28.cloned.1.call-done = bf16[128,704]{1,0:T(8,128)(2,1)} async-done(((bf16[1024,704]{1,0:T(8,128)(2,1)}), bf16[128,704]{1,0:T(8,128)(2,1)}) %reduce-scatter.28.cloned.1.call-update) | async-done | bytes 180240
  696.6 65.4 %reduce-scatter.30.cloned.1.call-done = bf16[128,704]{1,0:T(8,128)(2,1)} async-done(((bf16[1024,704]{1,0:T(8,128)(2,1)}), bf16[128,704]{1,0:T(8,128)(2,1)}) %reduce-scatter.30.cloned.1.call-update) | async-done | bytes 180240
  763.8 31.1 %reduce-scatter.18.cloned.1.call-done = bf16[1024,256]{1,0:T(8,128)(2,1)} async-done(((bf16[1024,1024]{1,0:T(8,128)(2,1)}), bf16[1024,256]{1,0:T(8,128)(2,1)}) %reduce-scatter.18.cloned.1.call-update) | async-done | bytes 524304 | tf_op jit(solution)/shard_map/reduce_scatter | solution.py:865
  797.1 75.7 %reduce-scatter.20.cloned.1.call-done = bf16[128,1536]{1,0:T(8,128)(2,1)} async-done(((bf16[1024,1536]{1,0:T(8,128)(2,1)}), bf16[128,1536]{1,0:T(8,128)(2,1)}) %reduce-scatter.20.cloned.1.call-update) | async-done | bytes 393232 | tf_op jit(solution)/shard_map/reduce_scatter | solution.py:911
  (150 shorter events, 60.9 us)
Async XLA Ops:
  7.2 11.7 %copy-start.35 = (f32[6]{0:T(128)S(1)}, f32[6]{0:T(128)}, u32[]{:S(2)}) copy-start(f32[6]{0:T(128)} %param.23) | copy-start | bytes 76
  7.2 34.1 %copy-start.26 = (f32[1024]{0:T(1024)S(1)}, f32[1024]{0:T(1024)}, u32[]{:S(2)}) copy-start(f32[1024]{0:T(1024)} %param.19) | copy-start | bytes 12292
  7.2 34.1 %copy-start.19 = (f32[4,1280]{1,0:T(4,128)S(1)}, f32[4,1280]{1,0:T(4,128)}, u32[]{:S(2)}) copy-start(f32[4,1280]{1,0:T(4,128)} %conv.3) | copy-start | bytes 61444
  7.2 34.1 %all-gather.6.cloned.1.call-start = ((), (), s32[]{:S(2)}) async-start(), calls=%async_computation.7 | async-start | bytes 2662400 | tf_op jit(solution)/shard_map/all_gather | solution.py:838
  8.0 6.2 collective-permute-start
  16.0 117.0 %all-gather.10.cloned.1.call-start = ((), (), s32[]{:S(2)}) async-start(), calls=%async_computation.14 | async-start | bytes 1179648 | tf_op jit(solution)/shard_map/all_gather | solution.py:856
  19.0 65.7 %copy-start.27 = (s32[4]{0:T(128)}, s32[4]{0:T(128)S(1)}, u32[]{:S(2)}) copy-start(s32[4]{0:T(128)S(1)} %pad_add_fusion.marks) | copy-start | bytes 52
  42.9 90.1 %copy-start.6 = (bf16[256,1024]{1,0:T(8,128)(2,1)S(1)}, bf16[256,1024]{1,0:T(8,128)(2,1)}, u32[]{:S(2)}) copy-start(bf16[256,1024]{1,0:T(8,128)(2,1)} %w_out.3) | copy-start | bytes 1572868
  42.9 90.1 %copy-start.29 = (f32[128]{0:T(128)S(1)}, f32[128]{0:T(128)}, u32[]{:S(2)}) copy-start(f32[128]{0:T(128)} %param.25) | copy-start | bytes 1540
  92.8 63.5 %all-gather.8.cloned.1.call-start = ((), (), s32[]{:S(2)}) async-start(), calls=%async_computation.9 | async-start | bytes 2621440 | tf_op jit(solution)/shard_map/all_gather | solution.py:841
  93.5 116.4 %all-reduce.9.cloned.1.call-start = ((), (), s32[]{:S(2)}) async-start(), calls=%async_computation.8 | async-start | bytes 4194304 | tf_op jit(solution)/shard_map/psum | solution.py:860
  140.3 142.5 %all-reduce.11.cloned.1.call-start = ((), (), s32[]{:S(2)}) async-start(), calls=%async_computation.11 | async-start | bytes 4194304 | tf_op jit(solution)/shard_map/psum | solution.py:864
  143.1 66.8 %copy-start.25 = (f32[1024]{0:T(1024)S(1)}, f32[1024]{0:T(1024)}, u32[]{:S(2)}) copy-start(f32[1024]{0:T(1024)} %param.27) | copy-start | bytes 12292
  231.2 209.9 %reduce-scatter.22.cloned.1.call-start = ((), (), s32[]{:S(2)}) async-start(), calls=%async_computation.15 | async-start | bytes 294912
  284.7 40.4 %copy-start.3 = (bf16[16,128,256]{2,1,0:T(8,128)(2,1)S(1)}, bf16[16,128,256]{2,1,0:T(8,128)(2,1)}, u32[]{:S(2)}) copy-start(bf16[16,128,256]{2,1,0:T(8,128)(2,1)} %all-gather.10.cloned.1.call-done) | copy-start | bytes 3145732
  284.7 40.4 %copy-start.12 = (f32[1024,256]{1,0:T(8,128)S(1)}, f32[1024,256]{1,0:T(8,128)}, u32[]{:S(2)}) copy-start(f32[1024,256]{1,0:T(8,128)} %copy-done.11) | copy-start | bytes 3145732
  284.7 40.4 %copy-start.18 = (f32[1024,128]{1,0:T(8,128)S(1)}, f32[1024,128]{1,0:T(8,128)}, u32[]{:S(2)}) copy-start(f32[1024,128]{1,0:T(8,128)} %copy-done.17) | copy-start | bytes 1572868
  284.7 40.4 %copy-start.20 = (f32[4,1280]{1,0:T(4,128)S(1)}, f32[4,1280]{1,0:T(4,128)}, u32[]{:S(2)}) copy-start(f32[4,1280]{1,0:T(4,128)} %conv.3) | copy-start | bytes 61444
  284.7 40.4 %copy-start.22 = (f32[8,1280]{1,0:T(8,128)S(1)}, f32[8,1280]{1,0:T(8,128)}, u32[]{:S(2)}) copy-start(f32[8,1280]{1,0:T(8,128)} %copy-done.21) | copy-start | bytes 122884
  284.7 40.4 %copy-start.28 = (s32[4]{0:T(128)S(1)}, s32[4]{0:T(128)}, u32[]{:S(2)}) copy-start(s32[4]{0:T(128)} %copy-done.27) | copy-start | bytes 52
  293.5 84.4 %copy-start.23 = (f32[8,1024]{1,0:T(8,128)}, f32[8,1024]{1,0:T(8,128)S(1)}, u32[]{:S(2)}) copy-start(f32[8,1024]{1,0:T(8,128)S(1)} %get-tuple-element.91) | copy-start | bytes 98308
  325.1 54.1 %copy-start.8 = (bf16[1024,1024]{1,0:T(8,128)(2,1)S(1)}, bf16[1024,1024]{1,0:T(8,128)(2,1)}, u32[]{:S(2)}) copy-start(bf16[1024,1024]{1,0:T(8,128)(2,1)} %copy-done.7) | copy-start | bytes 6291460
  377.9 7.9 collective-permute-start.1
  380.5 125.5 %reduce-scatter.24.cloned.1.call-start = ((), (), s32[]{:S(2)}) async-start(), calls=%async_computation.16 | async-start | bytes 589824
  385.7 173.2 %all-reduce.13.cloned.1.call-start = ((), (), s32[]{:S(2)}) async-start(), calls=%async_computation.12 | async-start | bytes 4194304 | tf_op jit(solution)/shard_map/psum | solution.py:894
  387.0 6.3 copy-start.34
  395.3 231.9 %reduce-scatter.26.cloned.1.call-start = ((), (), s32[]{:S(2)}) async-start(), calls=%async_computation.17 | async-start | bytes 1769472
  402.9 291.8 %reduce-scatter.28.cloned.1.call-start = ((), (), s32[]{:S(2)}) async-start(), calls=%async_computation.18 | async-start | bytes 1769472
  410.7 351.3 %reduce-scatter.30.cloned.1.call-start = ((), (), s32[]{:S(2)}) async-start(), calls=%async_computation.19 | async-start | bytes 1769472
  418.3 376.6 %reduce-scatter.18.cloned.1.call-start = ((), (), s32[]{:S(2)}) async-start(), calls=%async_computation.10 | async-start | bytes 2621440 | tf_op jit(solution)/shard_map/reduce_scatter | solution.py:865
  418.9 453.9 %reduce-scatter.20.cloned.1.call-start = ((), (), s32[]{:S(2)}) async-start(), calls=%async_computation.13 | async-start | bytes 3538944 | tf_op jit(solution)/shard_map/reduce_scatter | solution.py:911
  605.2 189.7 %slice-start = ((bf16[1040,1024]{1,0:T(8,128)(2,1)}), bf16[1024,1024]{1,0:T(8,128)(2,1)S(1)}, s32[]{:S(2)}) async-start(bf16[1040,1024]{1,0:T(8,128)(2,1)} %all-gather.6.cloned.1.call-done.x.x_halo), calls=%async_computation.20 | async-start | bytes 4194304 | tf_op jit(solution)/shard_map/slice | solution.py:870
  (20 other events, 22.8 us)
Sparse Core Ops, SparseCore 0:
  16.2 25.1 all-gather.5
  92.9 40.1 all-gather.9
  134.6 21.5 all-gather.7
  158.5 51.3 all-reduce.8
  231.3 51.4 all-reduce.10
  380.6 60.4 reduce-scatter.21
  445.0 60.9 reduce-scatter.23
  508.5 50.3 all-reduce.12
  562.3 64.8 reduce-scatter.25
  630.9 63.7 reduce-scatter.27
  698.2 63.7 reduce-scatter.29
  764.5 30.3 reduce-scatter.17
  798.5 74.2 reduce-scatter.19
